TPU v7x, 32 devices: a whole 2x2x4 slice. The times are simulated.
32 devices in a mesh: dp: 8 (over z, x), rep: 4 (over y, core).
Axes of the slice: x: 2, y: 2, z: 4, core: 2. Of those that a mesh axis runs over, the one named last changes fastest.
Arguments:
- features: bfloat16 [3, 20480, 2048], P(None, ('dp', 'rep')), may hold values from -6 to 6
- cotangent: bfloat16 [3, 20480, 2048], P(None, ('dp', 'rep')), may hold values from -6 to 6
- neighbours: int32 [3, 20480, 32], P(None, ('dp', 'rep')), may hold values from 0 to 127
- segments: int32 [3, 20480], P(None, ('dp', 'rep')), may hold values from 0 to 639, never falling along the last dimension, each value on 1 to 64 neighbouring positions
- live: int32 [3, 20480], P(None, ('dp', 'rep')), may hold values 0 or 1
- weight: bfloat16 [2048, 2048], P(('dp', 'rep')), may hold values from -0.125 to 0.125
- bias: bfloat16 [2048], P(('dp', 'rep')), may hold values from -3 to 3
Outputs:
- activations: bfloat16 [3, 20480, 2048], P(None, ('dp', 'rep'))
- feature_grad: bfloat16 [3, 20480, 2048], P(None, ('dp', 'rep'))
- weight_grad: float32 [2048, 2048], P(('dp', 'rep'))
- bias_grad: float32 [2048], P(('dp', 'rep'))
Inputs may be any that keep to these rules, and one draw needn't show every extreme that they name: `neighbours`: positions within the node's own slot of 128 nodes. `segments`: never falling along the nodes of a micro-batch; each cluster has 1 to 64 nodes, one exactly 64.
All inputs are finite; a program needn't handle non-finite values. No bound on the sum of `live` on one device may be relied on, other than what follows from the above.
Results may differ from a plain program's by a relative error of at most 0.0055.
Values may be sent and summed in bfloat16 or wider, within the bound.
A program may use at most 192 MiB of HBM per device.

v0:
```python
import functools

import jax
import jax.numpy as jnp
from jax import lax
from jax.experimental import pallas as pl
from jax.experimental.pallas import tpu as pltpu
from jax.sharding import PartitionSpec as P

SLOT = 128
LANES = 128
CHUNK = 256
MESH = pl.DeviceIdType.MESH
F32, BF16 = jnp.float32, jnp.bfloat16
ENHANCE = 1.0
LATE = 1
SLOTS = 6
LAST_GATHERED = (6, 7)


def split_axes(dp, rep):
    b = 2 ** ((dp.bit_length() - 1) // 2)
    return dp // b, b, rep // 2, 2


def feature_tile(dims, wg, gp, adj_t, scale, local, n, m):
    A, B, Y, C = dims
    chunks, rows = wg.shape[0], wg.shape[-2]
    wide = B * Y * C * rows
    slots = local // SLOT
    base = m * local if isinstance(m, int) else pl.multiple_of(m * local, local)
    w = jnp.concatenate([wg[k, h, n].reshape(wide, LANES) for k in range(chunks) for h in range(2)], axis=1)
    grad = lax.dot_general(gp[pl.ds(base, local), :], w, (((1,), (1,)), ((), ())), preferred_element_type=F32)
    grad = grad * jnp.concatenate([scale[pl.ds(base, local), :]] * (wide // LANES), axis=1)
    high = grad.astype(BF16)
    low = (grad - high.astype(F32)).astype(BF16)
    tiles = []
    for q in range(slots):
        left = adj_t[m * slots + q]
        part = slice(q * SLOT, (q + 1) * SLOT)
        right = jnp.concatenate([high[part], low[part]], axis=0)
        out = jnp.dot(jnp.concatenate([left, left], axis=1), right, preferred_element_type=F32)
        tiles.append(out.astype(BF16))
    return jnp.concatenate(tiles, axis=0)


def finish(
    dims, act, wg, gp, done, adj_t, scale, wout, bgrad_in, act_out, fgrad_out, wgrad_out, bgrad_out,
    fout, act_sem, done_sem, fout_sem, wout_sem,
):
    batches, local, D = fgrad_out.shape
    blocks, wide, early = dims[0], D // dims[0], batches - LATE

    def store(i):
        n, m = lax.div(i, LATE), early + lax.rem(i, LATE)
        cols = pl.ds(pl.multiple_of(n * wide, wide), wide)
        return pltpu.make_async_copy(fout.at[i], fgrad_out.at[m, :, cols], fout_sem.at[i])

    kept = [pltpu.make_async_copy(wout, wgrad_out, wout_sem.at[0])]
    for m in range(early):
        kept.append(pltpu.make_async_copy(done.at[pl.ds(m * local, local)], fgrad_out.at[m], done_sem.at[m]))
    for copy in kept:
        copy.start()
    for k in range(act.shape[0]):
        pltpu.make_async_copy(act.at[k], act_out.at[:, :, pl.ds(k * CHUNK, CHUNK)], act_sem.at[0]).start()
    bgrad_out[...] = bgrad_in[...]

    def step(i, carry):
        fout[i] = feature_tile(dims, wg, gp, adj_t, scale, local, lax.div(i, LATE), lax.rem(i, LATE))
        store(i).start()
        return carry

    lax.fori_loop(0, blocks * LATE, step, 0)
    for i in range(blocks * LATE):
        store(i).wait()
    pltpu.make_async_copy(act, act, act_sem.at[0]).wait()
    for copy in kept:
        copy.wait()


def kernel(
    dims, feat, cot, nbr, seg, live, weight, bias, act, wg, gp_l, pool_e, adj_l, scale_l, wout, bgrad_out,
    gp_e, pool_l, adj_e, scale_e, pool_t, ct, acc, csend, crecv, s1a, s1b, s2a, s2b, sz, r1a, r1b, r2a, r2b, rz,
    nbuf, sbuf, lbuf, bb, brow, bacc, bt, bsum, brc, br1, br2, brz,
    in_sem, ct_sem,
    gz_s, gz_r, g1a_s, g1a_r, g1b_s, g1b_r, g2a_s, g2a_r, g2b_s, g2b_r, gc_s, gc_r,
    rc_s, rc_r, p1a_s, p1a_r, p1b_s, p1b_r, p2a_s, p2a_r, p2b_s, p2b_r, pz_s, pz_r,
    bz_s, bz_r, b1_s, b1_r, b2_s, b2_r, bc_s, bc_r, dc_s, dc_r, d1_s, d1_r, d2_s, d2_r, dz_s, dz_r,
):
    A, B, Y, C = dims
    batches, local, D = feat.shape
    rows = weight.shape[0]
    slots = local // SLOT
    N = batches * local
    chunks = D // CHUNK
    groups = A * B * Y
    plane = groups * rows
    first = batches - LATE
    wide = D // A

    dp, rep = lax.axis_index("dp"), lax.axis_index("rep")
    a, b, y, c = lax.div(dp, B), lax.rem(dp, B), lax.div(rep, C), lax.rem(rep, C)
    oc = 1 - c

    def device(a_, b_, y_, c_):
        return (a_ * B + b_, y_ * C + c_)

    def columns(k):
        return pl.ds(k * CHUNK, CHUNK)

    def of(m, ref_e, ref_l):
        return (ref_e, m) if m < first else (ref_l, m - first)

    def rows_of(m, ref_e, ref_l):
        ref, at = of(m, ref_e, ref_l)
        return ref.at[pl.ds(at * local, local)]

    def up(v, d, n):
        return lax.rem(v + d, n)

    def down(v, d, n):
        return lax.rem(v + n - d, n)

    to_a = [(d, device(up(a, d, A), b, y, c)) for d in range(1, A)]
    to_b = [(d, device(a, up(b, d, B), y, c)) for d in range(1, B)]
    to_y = [(d, device(a, b, up(y, d, Y), c)) for d in range(1, Y)]
    to_c = device(a, b, y, oc)

    def remote(src, dst, ssem, rsem, dev):
        return pltpu.make_async_remote_copy(
            src_ref=src, dst_ref=dst, send_sem=ssem, recv_sem=rsem, device_id=dev, device_id_type=MESH
        )

    weight_loads = [
        pltpu.make_async_copy(
            weight.at[:, pl.ds((2 * k + h) * LANES, LANES)], wg.at[k, h, a, b, y, c], in_sem.at[0]
        )
        for k in range(chunks)
        for h in range(2)
    ]
    side_loads = [
        pltpu.make_async_copy(nbr, nbuf, in_sem.at[1]),
        pltpu.make_async_copy(seg, sbuf, in_sem.at[2]),
        pltpu.make_async_copy(live, lbuf, in_sem.at[3]),
    ]
    feat_loads = [
        pltpu.make_async_copy(feat.at[m], rows_of(m, gp_e, gp_l), in_sem.at[4 + m]) for m in range(batches)
    ]
    for copy in weight_loads:
        copy.start()
    for copy in side_loads:
        copy.start()
    for copy in feat_loads:
        copy.start()

    barrier = pltpu.get_barrier_semaphore()
    partners = [dev for _, dev in to_a + to_b + to_y] + [to_c]
    for dev in partners:
        pl.semaphore_signal(barrier, inc=1, device_id=dev, device_id_type=MESH)

    def cot_load(k):
        return pltpu.make_async_copy(cot.at[:, :, columns(k)], ct.at[k % 2], ct_sem.at[k % 2])

    pl.semaphore_wait(barrier, len(partners))

    def gather_z(k, d, dev):
        ref = wg.at[k, :, a, b, y, c]
        return remote(ref, ref, gz_s.at[0], gz_r.at[k], dev)

    def gather_1(k, mine):
        out = []
        for d, dev in to_b:
            ref = wg.at[k, 0, :, b if mine else down(b, d, B), y, c]
            out.append(remote(ref, ref, g1a_s.at[0, d - 1], g1a_r.at[k, d - 1], dev))
        for d, dev in to_y:
            ref = wg.at[k, 1, :, b, y if mine else down(y, d, Y), c]
            out.append(remote(ref, ref, g1b_s.at[0, d - 1], g1b_r.at[k, d - 1], dev))
        return out

    def gather_2(k, mine):
        out = []
        for d, dev in to_y:
            ref = wg.at[k, 0, :, :, y if mine else down(y, d, Y), c]
            out.append(remote(ref, ref, g2a_s.at[0, d - 1], g2a_r.at[k, d - 1], dev))
        for d, dev in to_b:
            ref = wg.at[k, 1, :, b if mine else down(b, d, B), :, c]
            out.append(remote(ref, ref, g2b_s.at[0, d - 1], g2b_r.at[k, d - 1], dev))
        return out

    def turned_1(k, mine):
        out = []
        for d, dev in to_b:
            ref = wg.at[k, 0, a, b if mine else down(b, d, B), y, c]
            out.append(remote(ref, ref, g1a_s.at[1, d - 1], g1a_r.at[k, d - 1], dev))
        for d, dev in to_y:
            ref = wg.at[k, 1, a, b, y if mine else down(y, d, Y), c]
            out.append(remote(ref, ref, g1b_s.at[1, d - 1], g1b_r.at[k, d - 1], dev))
        return out

    def turned_2(k, mine):
        out = []
        for d, dev in to_y:
            ref = wg.at[k, 0, a, :, y if mine else down(y, d, Y), c]
            out.append(remote(ref, ref, g2a_s.at[1, d - 1], g2a_r.at[k, d - 1], dev))
        for d, dev in to_b:
            ref = wg.at[k, 1, a, b if mine else down(b, d, B), :, c]
            out.append(remote(ref, ref, g2b_s.at[1, d - 1], g2b_r.at[k, d - 1], dev))
        return out

    def turned_z(k):
        out = []
        ref = wg.at[k, :, a, :, :, c]
        for d, dev in to_a:
            out.append(remote(ref, ref, gz_s.at[1], gz_r.at[k], dev))
        return out

    def gather_c(k, mine):
        ref = wg.at[k, :, :, :, :, c if mine else oc]
        return remote(ref, ref, gc_s.at[0], gc_r.at[k], to_c)

    def region(fn):
        pl.when(dp >= 0)(fn)

    def bias_z(d, dev):
        ref = bb.at[a, b, y, c]
        return remote(ref, ref, bz_s.at[0], bz_r.at[0], dev)

    def bias_1(d, dev, mine):
        ref = bb.at[:, b if mine else down(b, d, B), y, c]
        return remote(ref, ref, b1_s.at[d - 1], b1_r.at[d - 1], dev)

    def bias_2(d, dev, mine):
        ref = bb.at[:, :, y if mine else down(y, d, Y), c]
        return remote(ref, ref, b2_s.at[d - 1], b2_r.at[d - 1], dev)

    def bias_c(mine):
        ref = bb.at[:, :, :, c if mine else oc]
        return remote(ref, ref, bc_s.at[0], bc_r.at[0], to_c)

    def ag1(k):
        every = wg.at[k, :, : A - 1, b, y, c]
        remote(every, every, gz_s.at[0], gz_r.at[k], to_c).wait_recv()
        for copy in gather_1(k, True):
            copy.start()

    def ag2(k):
        for copy in gather_1(k, False):
            copy.wait_recv()
        for copy in gather_2(k, True):
            copy.start()

    def ag3(k):
        for copy in gather_2(k, False):
            copy.wait_recv()
        gather_c(k, True).start()

    def at1(k):
        for copy in turned_1(k, True):
            copy.start()

    def at2(k):
        for copy in turned_1(k, False):
            copy.wait_recv()
        for copy in turned_2(k, True):
            copy.start()

    def atz(k):
        for copy in turned_2(k, False):
            copy.wait_recv()
        for copy in turned_z(k):
            copy.start()

    def at3(k):
        every = wg.at[k, :, : A - 1, :, :, c]
        remote(every, every, gz_s.at[1], gz_r.at[k], to_c).wait_recv()
        gather_c(k, True).start()

    def bias_ag1():
        every = bb.at[: A - 1, b, y, c]
        remote(every, every, bz_s.at[0], bz_r.at[0], to_c).wait_recv()
        for d, dev in to_b:
            bias_1(d, dev, True).start()

    def bias_ag2():
        for d, dev in to_b:
            bias_1(d, dev, False).wait_recv()
        for d, dev in to_y:
            bias_2(d, dev, True).start()

    def bias_ag3():
        for d, dev in to_y:
            bias_2(d, dev, False).wait_recv()
        bias_c(True).start()

    def agz(k):
        for d, dev in to_a:
            gather_z(k, d, dev).start()

    def bias_agz():
        spread = lax.rem(lax.broadcasted_iota(jnp.int32, (rows, LANES), 1), rows)
        spread = (spread == lax.broadcasted_iota(jnp.int32, (rows, LANES), 0)).astype(F32).astype(BF16)
        own_bias = jnp.broadcast_to(bias[...], (8, rows))
        bb[a, b, y, c] = jnp.dot(own_bias, spread, preferred_element_type=F32)
        for d, dev in to_a:
            bias_z(d, dev).start()

    pltpu.make_async_copy(weight, weight, in_sem.at[0]).wait()
    bias_agz()
    agz(0)
    for k in LAST_GATHERED:
        at1(k)

    for copy in side_loads:
        copy.wait()
    cot_load(0).start()
    bacc[...] = jnp.zeros_like(bacc)

    def pooling(m, q):
        here = pl.multiple_of(q * SLOT, SLOT)
        flat = pl.multiple_of((m * slots + q) * SLOT, SLOT)
        listed = nbuf[m, :, pl.ds(here, SLOT)].astype(F32).astype(BF16)
        lane = lax.broadcasted_iota(jnp.int32, (SLOT, SLOT), 1)
        sub = lax.broadcasted_iota(jnp.int32, (SLOT, SLOT), 0)
        position = sub.astype(F32).astype(BF16)
        counted = jnp.zeros((SLOT, SLOT), BF16)
        for j in range(listed.shape[0]):
            counted = counted + jnp.where(listed[j : j + 1, :] == position, jnp.bfloat16(1), jnp.bfloat16(0))
        counted = counted.astype(F32).T
        ids, alive = sbuf[m : m + 1, pl.ds(here, SLOT)], lbuf[m : m + 1, pl.ds(here, SLOT)]
        along = jnp.where(alive > 0, ids, -1)
        down_ = jnp.broadcast_to(jnp.where(alive > 0, ids, -2), (SLOT, SLOT)).T
        adjacency = jnp.where(down_ == along, counted, 0.0)
        degree = jnp.sum(adjacency, axis=1, keepdims=True)
        factor = jnp.where(down_ >= 0, 1.0 / (degree + 1.0), 0.0)
        adjacency = jnp.where(lane == sub, (1.0 + ENHANCE) * (adjacency + 1.0), adjacency)
        adj, at = of(m, adj_e, adj_l)
        adj[at * slots + q] = adjacency.T.astype(BF16)
        rows_of(m, scale_e, scale_l)[pl.ds(here, SLOT), :] = factor
        block = rows_of(m, gp_e, gp_l)[pl.ds(here, SLOT), :]
        pooled = jnp.dot(adjacency.astype(BF16), block, preferred_element_type=F32)
        pooled = (pooled * jnp.concatenate([factor] * (D // SLOT), axis=1)).astype(BF16)
        rows_of(m, pool_e, pool_l)[pl.ds(here, SLOT), :] = pooled
        pool_t[:, :, :, pl.ds(flat, SLOT)] = pooled.T.reshape(groups, C, rows, SLOT)

    early = {
        2: [lambda: agz(1)],
        4: [bias_ag1, lambda: ag1(0)],
        6: [lambda: at2(6), lambda: at2(7), lambda: agz(2)],
        10: [bias_ag2, lambda: ag2(0), lambda: ag1(1), lambda: agz(3)],
    }
    for m in range(batches):
        feat_loads[m].wait()

        def step(q, carry, m=m):
            pooling(m, q)
            for at, events in early.items():
                if m * slots <= at < (m + 1) * slots:

                    @pl.when(q == at - m * slots)
                    def _(events=events):
                        for event in events:
                            event()

            return carry

        lax.fori_loop(0, slots, step, 0)

    agz(4)
    ag1(2)
    bias_ag3()
    ag3(0)
    agz(5)

    bias_c(False).wait_recv()
    tiles = bb[...].reshape(groups * C, 8, LANES)
    per = LANES // rows
    owner = lax.div(lax.broadcasted_iota(jnp.int32, (1, LANES), 1), rows)
    for j in range(D // LANES):
        row = jnp.zeros((1, LANES), F32)
        for p in range(per):
            row = jnp.where(owner == p, tiles[j * per + p, 0:1, :], row)
        brow[j] = jnp.broadcast_to(row, (8, LANES))

    def reduce_c(k):
        return remote(csend.at[k % 2], crecv.at[k], rc_s.at[k % 2], rc_r.at[k], to_c)

    def reduce_1(k):
        e = k % 2
        out_a = [
            remote(s1a.at[e, d - 1], r1a.at[k, d - 1], p1a_s.at[e, d - 1], p1a_r.at[k, d - 1], dev) for d, dev in to_y
        ]
        out_b = [
            remote(s1b.at[e, d - 1], r1b.at[k, d - 1], p1b_s.at[e, d - 1], p1b_r.at[k, d - 1], dev) for d, dev in to_b
        ]
        return out_a + out_b

    def reduce_2(k):
        e = k % 2
        out_a = [
            remote(s2a.at[e, d - 1], r2a.at[k, d - 1], p2a_s.at[e, d - 1], p2a_r.at[k, d - 1], dev) for d, dev in to_b
        ]
        out_b = [
            remote(s2b.at[e, d - 1], r2b.at[k, d - 1], p2b_s.at[e, d - 1], p2b_r.at[k, d - 1], dev) for d, dev in to_y
        ]
        return out_a + out_b

    def reduce_z(k):
        e = k % 2
        return [remote(sz.at[e, d - 1], rz.at[k, d - 1], pz_s.at[e], pz_r.at[k], dev) for d, dev in to_a]

    def reduce_z_sent(k):
        remote(sz.at[k % 2], rz.at[k], pz_s.at[k % 2], pz_r.at[k], to_c).wait_send()

    def ago(k, n, copies):
        if k >= n:
            for copy in copies(k - n):
                copy.wait_send()

    lo, hi = slice(0, LANES), slice(LANES, CHUNK)

    def rs1(k):
        t, e = k % SLOTS, k % 2
        reduce_c(k).wait_recv()
        ago(k, 2, reduce_1)
        for d, _ in to_y:
            v = up(y, d, Y)
            s1a[e, d - 1] = (acc[t, :, :, v, :, lo] + crecv[k, :, :, v, :, lo].astype(F32)).astype(BF16)
        for d, _ in to_b:
            v = up(b, d, B)
            s1b[e, d - 1] = (acc[t, :, v, :, :, hi] + crecv[k, :, v, :, :, hi].astype(F32)).astype(BF16)
        for copy in reduce_1(k):
            copy.start()
        acc[t, :, :, y, :, lo] = acc[t, :, :, y, :, lo] + crecv[k, :, :, y, :, lo].astype(F32)
        acc[t, :, b, :, :, hi] = acc[t, :, b, :, :, hi] + crecv[k, :, b, :, :, hi].astype(F32)

    def rs2(k):
        t, e = k % SLOTS, k % 2
        for copy in reduce_1(k):
            copy.wait_recv()
        ago(k, 2, reduce_2)

        def total_a(v):
            out = acc[t, :, v, y, :, lo]
            for d, _ in to_y:
                out = out + r1a[k, d - 1, :, v].astype(F32)
            return out

        def total_b(v):
            out = acc[t, :, b, v, :, hi]
            for d, _ in to_b:
                out = out + r1b[k, d - 1, :, v].astype(F32)
            return out

        for d, _ in to_b:
            s2a[e, d - 1] = total_a(up(b, d, B)).astype(BF16)
        for d, _ in to_y:
            s2b[e, d - 1] = total_b(up(y, d, Y)).astype(BF16)
        for copy in reduce_2(k):
            copy.start()
        acc[t, :, b, y, :, lo] = total_a(b)
        acc[t, :, b, y, :, hi] = total_b(y)

    def rs3(k):
        t, e = k % SLOTS, k % 2
        for copy in reduce_2(k):
            copy.wait_recv()
        if k >= 2:
            reduce_z_sent(k - 2)

        def total(v):
            left, right = acc[t, v, b, y, :, lo], acc[t, v, b, y, :, hi]
            for d, _ in to_b:
                left = left + r2a[k, d - 1, v].astype(F32)
            for d, _ in to_y:
                right = right + r2b[k, d - 1, v].astype(F32)
            return jnp.concatenate([left, right], axis=1)

        for d, _ in to_a:
            sz[e, d - 1] = total(up(a, d, A)).astype(BF16)
        for copy in reduce_z(k):
            copy.start()
        acc[t, a, b, y] = total(a)

    def rs4(k):
        t = k % SLOTS
        remote(sz.at[k % 2], rz.at[k], pz_s.at[k % 2], pz_r.at[k], to_c).wait_recv()
        out = acc[t, a, b, y]
        for d, _ in to_a:
            out = out + rz[k, d - 1].astype(F32)
        wout[:, columns(k)] = out

    def bred_c():
        return remote(bt.at[:, :, :, oc], brc, dc_s.at[0], dc_r.at[0], to_c)

    def bred_1():
        return [remote(bsum.at[:, :, up(y, d, Y)], br1.at[d - 1], d1_s.at[d - 1], d1_r.at[d - 1], dev) for d, dev in to_y]

    def bred_2():
        return [remote(bsum.at[:, up(b, d, B), y], br2.at[d - 1], d2_s.at[d - 1], d2_r.at[d - 1], dev) for d, dev in to_b]

    def bred_z():
        return [remote(bsum.at[up(a, d, A), b, y], brz.at[d - 1], dz_s.at[0], dz_r.at[0], dev) for d, dev in to_a]

    def bias_rs0():
        for a_ in range(A):
            for b_ in range(B):
                for y_ in range(Y):
                    for c_ in range(C):
                        block = (((a_ * B + b_) * Y + y_) * C + c_) * rows // LANES
                        bt[a_, b_, y_, c_] = bacc[:, block * LANES : (block + 1) * LANES]
        bred_c().start()

    def bias_rs1():
        bred_c().wait_recv()
        bsum[...] = bt[:, :, :, c] + brc[...]
        for copy in bred_1():
            copy.start()

    def bias_rs2():
        for copy in bred_1():
            copy.wait_recv()
        for d, _ in to_y:
            bsum[:, :, y] = bsum[:, :, y] + br1[d - 1]
        for copy in bred_2():
            copy.start()

    def bias_rs3():
        for copy in bred_2():
            copy.wait_recv()
        for d, _ in to_b:
            bsum[:, b, y] = bsum[:, b, y] + br2[d - 1]
        for copy in bred_z():
            copy.start()

    def bias_rs4():
        remote(brz, brz, dz_s.at[0], dz_r.at[0], to_c).wait_recv()
        out = bsum[a, b, y]
        for d, _ in to_a:
            out = out + brz[d - 1]
        out = jnp.sum(out, axis=0, keepdims=True)
        place = lax.rem((dp * (Y * C) + rep) * rows, LANES)
        mine = jnp.zeros((1, rows), F32)
        for p in range(per):
            mine = jnp.where(place == p * rows, out[:, p * rows : (p + 1) * rows], mine)
        bgrad_out[...] = mine

    def forward(k):
        e = k % 2
        w = jnp.concatenate([wg[k, h].reshape(D, LANES) for h in range(2)], axis=1)
        offset = jnp.concatenate([brow[2 * k + h][0:1] for h in range(2)], axis=1)
        sums = jnp.zeros((8, CHUNK), F32)
        for m in range(batches):
            preact = jnp.dot(rows_of(m, pool_e, pool_l)[...], w, preferred_element_type=F32) + offset
            squash = jax.nn.sigmoid(preact)
            active = preact * squash
            act[k, m] = active.astype(BF16)
            grad = (ct[e, m].astype(F32) * (squash + active * (1.0 - squash))).astype(BF16)
            rows_of(m, gp_e, gp_l)[:, columns(k)] = grad
            sums = sums + jnp.sum(grad.astype(F32).reshape(local // 8, 8, CHUNK), axis=0)
        bacc[:, columns(k)] = sums

    def weight_term(k, which):
        left = pool_t[:, which].reshape(plane, N)
        right = jnp.concatenate([gp_e[:, columns(k)], gp_l[:, columns(k)]], axis=0)
        return jnp.dot(left, right, preferred_element_type=F32).reshape(A, B, Y, rows, CHUNK)

    def forward_region(k):
        gather_c(k, False).wait_recv()
        cot_load(k).wait()
        if k + 1 < chunks:
            cot_load(k + 1).start()

    def weight_region(k):
        if k >= 2:
            reduce_c(k - 2).wait_send()

    def weight_terms(k):
        csend[k % 2] = weight_term(k, oc).astype(BF16)
        acc[k % SLOTS] = weight_term(k, c)

    regions = [(0, None), (None, 0), (1, None), (None, 1), (2, None)]
    regions += [(k, k - 1) for k in range(3, chunks)] + [(None, chunks - 1)]
    plan = [
        (lambda _: bias_rs0(), {0: 10}),
        (lambda _: bias_rs1(), {0: 11}),
        (ag2, {1: 0, 2: 1, 3: 2, 4: 3, 5: 5}),
        (ag1, {3: 0, 4: 1, 5: 3}),
        (ag3, {1: 1, 2: 3, 3: 4, 4: 5, 5: 6}),
        (at3, {6: 7, 7: 8}),
        (atz, {6: 0, 7: 4}),
        (rs4, {0: 9, 1: 10}),
        (rs3, {0: 8, 1: 9, 2: 10}),
        (rs2, {0: 7, 1: 8, 2: 9, 3: 10, 4: 11}),
        (rs1, {0: 5, 1: 6, 2: 7, 3: 8, 4: 9, 5: 10, 6: 11}),
    ]
    regions.append((None, None))
    for at, (f, w) in enumerate(regions):
        for stage, when in plan:
            for k, ahead in when.items():
                if ahead == at:
                    stage(k)
        if f is not None:
            forward_region(f)
        if w is not None:
            weight_region(w)
        if f is None and w is None:
            continue

        @region
        def _(f=f, w=w):
            if f is not None:
                forward(f)
            if w is not None:
                weight_terms(w)

        if w is not None:
            reduce_c(w).start()

    def feature_grad(i):
        n, m = lax.div(i, first), lax.rem(i, first)
        part, cols = pl.ds(pl.multiple_of(m * local, local), local), pl.ds(pl.multiple_of(n * wide, wide), wide)
        pool_e[part, cols] = feature_tile(dims, wg, gp_e, adj_e, scale_e, local, n, m)

    late = [
        (rs1, {7: 0}),
        (lambda _: bias_rs2(), {0: 1}),
        (rs2, {5: 1, 6: 2, 7: 4}),
        (rs3, {3: 0, 4: 2, 5: 4, 6: 5, 7: 6}),
        (lambda _: bias_rs3(), {0: 5}),
        (rs4, {2: 1, 3: 3, 4: 5, 5: 7, 6: 7, 7: 7}),
        (lambda _: bias_rs4(), {0: 7}),
    ]

    def last(i, carry):
        pl.when(i >= 0)(lambda: feature_grad(i))
        for stage, when in late:
            for k, at in when.items():
                pl.when(i == at)(functools.partial(stage, k))
        return carry

    lax.fori_loop(0, A * first, last, 0)

    for k in (chunks - 2, chunks - 1):
        for copy in [reduce_c(k)] + reduce_1(k) + reduce_2(k):
            copy.wait_send()
        reduce_z_sent(k)

    def drained(ref, sem, dev):
        remote(ref, ref, sem, sem, dev).wait_send()

    plain, turned = slice(0, LAST_GATHERED[0]), slice(LAST_GATHERED[0], chunks)
    drained(wg.at[plain, :, : A - 1, b, y, c], gz_s.at[0], to_c)
    drained(wg.at[turned, :, : A - 1, :, :, c], gz_s.at[1], to_c)
    for d, dev in to_b:
        drained(wg.at[plain, 0, :, b, y, c], g1a_s.at[0, d - 1], dev)
        drained(wg.at[plain, 1, :, b, :, c], g2b_s.at[0, d - 1], dev)
        drained(wg.at[turned, 0, a, b, y, c], g1a_s.at[1, d - 1], dev)
        drained(wg.at[turned, 1, a, b, :, c], g2b_s.at[1, d - 1], dev)
    for d, dev in to_y:
        drained(wg.at[plain, 1, :, b, y, c], g1b_s.at[0, d - 1], dev)
        drained(wg.at[plain, 0, :, :, y, c], g2a_s.at[0, d - 1], dev)
        drained(wg.at[turned, 1, a, b, y, c], g1b_s.at[1, d - 1], dev)
        drained(wg.at[turned, 0, a, :, y, c], g2a_s.at[1, d - 1], dev)
    drained(wg.at[:, :, :, :, :, c], gc_s.at[0], to_c)
    drained(bb.at[: A - 1, b, y, c], bz_s.at[0], to_c)
    for d, dev in to_b:
        bias_1(d, dev, True).wait_send()
    for d, dev in to_y:
        bias_2(d, dev, True).wait_send()
    bias_c(True).wait_send()
    for copy in [bred_c()] + bred_1() + bred_2():
        copy.wait_send()
    drained(brz, dz_s.at[0], to_c)


def per_device(dims, features, cotangent, neighbours, segments, live, weight, bias):
    A, B, Y, C = dims
    batches, local, D = features.shape
    rows = weight.shape[0]
    N = batches * local
    N_l = LATE * local
    N_e = N - N_l
    chunks = D // CHUNK
    groups = A * B * Y
    wide = D // A
    neighbours = jnp.swapaxes(neighbours, 1, 2)
    any_spec = pl.BlockSpec(memory_space=pl.ANY)
    vmem, dma = pltpu.VMEM, pltpu.SemaphoreType.DMA
    scratch = [
        vmem((N_e, D), BF16),
        vmem((N_l, D), BF16),
        vmem((N_e // SLOT, SLOT, SLOT), BF16),
        vmem((N_e, SLOT), F32),
        vmem((groups, C, rows, N), BF16),
        vmem((2, batches, local, CHUNK), BF16),
        vmem((SLOTS, A, B, Y, rows, CHUNK), F32),
        vmem((2, A, B, Y, rows, CHUNK), BF16),
        vmem((chunks, A, B, Y, rows, CHUNK), BF16),
        vmem((2, Y - 1, A, B, rows, LANES), BF16),
        vmem((2, B - 1, A, Y, rows, LANES), BF16),
        vmem((2, B - 1, A, rows, LANES), BF16),
        vmem((2, Y - 1, A, rows, LANES), BF16),
        vmem((2, A - 1, rows, CHUNK), BF16),
        vmem((chunks, Y - 1, A, B, rows, LANES), BF16),
        vmem((chunks, B - 1, A, Y, rows, LANES), BF16),
        vmem((chunks, B - 1, A, rows, LANES), BF16),
        vmem((chunks, Y - 1, A, rows, LANES), BF16),
        vmem((chunks, A - 1, rows, CHUNK), BF16),
        vmem(neighbours.shape, jnp.int32),
        vmem(segments.shape, jnp.int32),
        vmem(live.shape, jnp.int32),
        vmem((A, B, Y, C, 8, LANES), F32),
        vmem((D // LANES, 8, LANES), F32),
        vmem((8, D), F32),
        vmem((A, B, Y, C, 8, LANES), F32),
        vmem((A, B, Y, 8, LANES), F32),
        vmem((A, B, Y, 8, LANES), F32),
        vmem((Y - 1, A, B, 8, LANES), F32),
        vmem((B - 1, A, 8, LANES), F32),
        vmem((A - 1, 8, LANES), F32),
        dma((4 + batches,)),
        dma((2,)),
    ]
    for sent, received in (
        ((2,), (chunks,)),
        ((2, B - 1), (chunks, B - 1)),
        ((2, Y - 1), (chunks, Y - 1)),
        ((2, Y - 1), (chunks, Y - 1)),
        ((2, B - 1), (chunks, B - 1)),
        ((1,), (chunks,)),
        ((2,), (chunks,)),
        ((2, Y - 1), (chunks, Y - 1)),
        ((2, B - 1), (chunks, B - 1)),
        ((2, B - 1), (chunks, B - 1)),
        ((2, Y - 1), (chunks, Y - 1)),
        ((2,), (chunks,)),
        ((1,), (1,)),
        ((B - 1,), (B - 1,)),
        ((Y - 1,), (Y - 1,)),
        ((1,), (1,)),
        ((1,), (1,)),
        ((Y - 1,), (Y - 1,)),
        ((B - 1,), (B - 1,)),
        ((1,), (1,)),
    ):
        scratch += [dma(sent), dma(received)]
    vmem_spec = pl.BlockSpec(memory_space=pltpu.VMEM)
    kept = [
        vmem((chunks, batches, local, CHUNK), BF16),
        vmem((chunks, 2, A, B, Y, C, rows, LANES), BF16),
        vmem((N_l, D), BF16),
        vmem((N_e, D), BF16),
        vmem((N_l // SLOT, SLOT, SLOT), BF16),
        vmem((N_l, SLOT), F32),
        vmem((rows, D), F32),
        vmem((1, rows), F32),
    ]
    kept_arrays = pl.pallas_call(
        functools.partial(kernel, dims),
        out_shape=kept,
        in_specs=[any_spec] * 6 + [vmem_spec],
        out_specs=[vmem_spec] * len(kept),
        scratch_shapes=scratch,
        compiler_params=pltpu.CompilerParams(
            collective_id=0, has_side_effects=True, vmem_limit_bytes=39 * 2**20
        ),
        cost_estimate=pl.CostEstimate(
            flops=6 * N * D * D, bytes_accessed=8 * N * D, transcendentals=N * D
        ),
    )(features, cotangent, neighbours, segments, live, weight, bias.reshape(1, rows))
    act, fgrad, wgrad, bgrad = pl.pallas_call(
        functools.partial(finish, dims),
        out_shape=[
            jax.ShapeDtypeStruct(features.shape, BF16),
            jax.ShapeDtypeStruct(features.shape, BF16),
            jax.ShapeDtypeStruct(weight.shape, F32),
            jax.ShapeDtypeStruct((1, rows), F32),
        ],
        in_specs=[vmem_spec] * len(kept),
        out_specs=[any_spec] * 3 + [vmem_spec],
        scratch_shapes=[
            vmem((A * LATE, local, wide), BF16),
            dma((1,)), dma((batches - LATE,)), dma((A * LATE,)), dma((1,)),
        ],
        compiler_params=pltpu.CompilerParams(vmem_limit_bytes=8 * 2**20),
    )(
        *[pltpu.with_memory_space_constraint(x, pltpu.VMEM) for x in kept_arrays],
    )
    return act, fgrad, wgrad, bgrad.reshape(rows)


def solution(mesh):
    both = ("dp", "rep")
    dims = split_axes(mesh.shape["dp"], mesh.shape["rep"])
    return jax.shard_map(
        functools.partial(per_device, dims),
        mesh=mesh,
        in_specs=(
            P(None, both, None), P(None, both, None), P(None, both, None),
            P(None, both), P(None, both), P(both, None), P(both),
        ),
        out_specs=(P(None, both, None), P(None, both, None), P(both, None), P(both)),
        check_vma=False,
    )
```

profile of v0, /device:TPU:0, one launch (start us, length us, event | category | flops | bytes accessed | tf_op | source)
XLA Modules:
  0.0 99.2 jit_solution(12125056115974658641)
XLA Ops:
  0.6 89.9 %shard_map.102 = (bf16[8,3,640,256]{3,2,1,0:T(8,128)(2,1)S(1)}, bf16[8,2,4,2,2,2,64,128]{7,6,5,4,3,2,1,0:T(8,128)(2,1)S(1)}, bf16[640,2048]{1,0:T(8,128)(2,1)S(1...) custom-call(bf16[3,640,2048]{2,1,0:T(8,128)(2,1)} %feat.1, ...), custom_call_target="tpu_custom_call" | custom-call | flops 48318382080 | bytes 31457280 | tf_op jit(solution)/shard_map/pallas_call | solution.py:758
  90.6 8.4 %shard_map.103 = (bf16[3,640,2048]{2,1,0:T(8,128)(2,1)}, bf16[3,640,2048]{2,1,0:T(8,128)(2,1)}, f32[64,2048]{1,0:T(8,128)}, f32[1,64]{1,0:T(1,128)}) custom-call(bf16[8,3,640,256]{3,2,1,0:T(8,128)(2,1)S(1)} %get-tuple-element.16.act, bf16[8,2,4,2,2,2,64,128]{7,6,5,4,3,2,1,0:T(8,128)(2,1)S(1)} %get-tuple-element.17.wg, ...), custom_call_target="tpu_custom_call" | custom-call | tf_op jit(solution)/shard_map/pallas_call | solution.py:771
where the time goes:
time: 99.4 us; the launch traced here: 99.2 us
  Pallas kernels  98.4 us (99%)
    pallas_call x1, Pallas kernels, per_device(): pl.pallas_call(functools.partial(kernel, dims), out_shape=kept, in_specs=...  89.9 us
    pallas_call x1, Pallas kernels, per_device(): pl.pallas_call(functools.partial(finish, dims), out_shape=[jax.ShapeDtype...  8.41 us

commit v1 on v0

--- a/solution.py
+++ b/solution.py
@@ -14,7 +14,7 @@
 F32, BF16 = jnp.float32, jnp.bfloat16
 ENHANCE = 1.0
 LATE = 1
-SLOTS = 6
+SLOTS, RECEIVED = 7, 6
 LAST_GATHERED = (6, 7)
 
 
@@ -106,7 +106,7 @@
         return (a_ * B + b_, y_ * C + c_)
 
     def columns(k):
-        return pl.ds(k * CHUNK, CHUNK)
+        return pl.ds(k * CHUNK if isinstance(k, int) else pl.multiple_of(k * CHUNK, CHUNK), CHUNK)
 
     def of(m, ref_e, ref_l):
         return (ref_e, m) if m < first else (ref_l, m - first)
@@ -382,7 +382,7 @@
         brow[j] = jnp.broadcast_to(row, (8, LANES))
 
     def reduce_c(k):
-        return remote(csend.at[k % 2], crecv.at[k], rc_s.at[k % 2], rc_r.at[k], to_c)
+        return remote(csend.at[k % 2], crecv.at[k % RECEIVED], rc_s.at[k % 2], rc_r.at[k], to_c)
 
     def reduce_1(k):
         e = k % 2
@@ -424,14 +424,14 @@
         ago(k, 2, reduce_1)
         for d, _ in to_y:
             v = up(y, d, Y)
-            s1a[e, d - 1] = (acc[t, :, :, v, :, lo] + crecv[k, :, :, v, :, lo].astype(F32)).astype(BF16)
+            s1a[e, d - 1] = (acc[t, :, :, v, :, lo] + crecv[k % RECEIVED, :, :, v, :, lo].astype(F32)).astype(BF16)
         for d, _ in to_b:
             v = up(b, d, B)
-            s1b[e, d - 1] = (acc[t, :, v, :, :, hi] + crecv[k, :, v, :, :, hi].astype(F32)).astype(BF16)
+            s1b[e, d - 1] = (acc[t, :, v, :, :, hi] + crecv[k % RECEIVED, :, v, :, :, hi].astype(F32)).astype(BF16)
         for copy in reduce_1(k):
             copy.start()
-        acc[t, :, :, y, :, lo] = acc[t, :, :, y, :, lo] + crecv[k, :, :, y, :, lo].astype(F32)
-        acc[t, :, b, :, :, hi] = acc[t, :, b, :, :, hi] + crecv[k, :, b, :, :, hi].astype(F32)
+        acc[t, :, :, y, :, lo] = acc[t, :, :, y, :, lo] + crecv[k % RECEIVED, :, :, y, :, lo].astype(F32)
+        acc[t, :, b, :, :, hi] = acc[t, :, b, :, :, hi] + crecv[k % RECEIVED, :, b, :, :, hi].astype(F32)
 
     def rs2(k):
         t, e = k % SLOTS, k % 2
@@ -544,12 +544,12 @@
             mine = jnp.where(place == p * rows, out[:, p * rows : (p + 1) * rows], mine)
         bgrad_out[...] = mine
 
-    def forward(k):
+    def forward(k, parts):
         e = k % 2
         w = jnp.concatenate([wg[k, h].reshape(D, LANES) for h in range(2)], axis=1)
         offset = jnp.concatenate([brow[2 * k + h][0:1] for h in range(2)], axis=1)
         sums = jnp.zeros((8, CHUNK), F32)
-        for m in range(batches):
+        for m in parts:
             preact = jnp.dot(rows_of(m, pool_e, pool_l)[...], w, preferred_element_type=F32) + offset
             squash = jax.nn.sigmoid(preact)
             active = preact * squash
@@ -557,7 +557,7 @@
             grad = (ct[e, m].astype(F32) * (squash + active * (1.0 - squash))).astype(BF16)
             rows_of(m, gp_e, gp_l)[:, columns(k)] = grad
             sums = sums + jnp.sum(grad.astype(F32).reshape(local // 8, 8, CHUNK), axis=0)
-        bacc[:, columns(k)] = sums
+        bacc[:, columns(k)] = sums if parts[0] == 0 else bacc[:, columns(k)] + sums
 
     def weight_term(k, which):
         left = pool_t[:, which].reshape(plane, N)
@@ -567,54 +567,87 @@
     def forward_region(k):
         gather_c(k, False).wait_recv()
         cot_load(k).wait()
-        if k + 1 < chunks:
+        if not isinstance(k, int) or k + 1 < chunks:
             cot_load(k + 1).start()
 
     def weight_region(k):
         if k >= 2:
             reduce_c(k - 2).wait_send()
 
-    def weight_terms(k):
+    def weight_other(k):
         csend[k % 2] = weight_term(k, oc).astype(BF16)
+
+    def weight_own(k):
         acc[k % SLOTS] = weight_term(k, c)
 
+    whole = list(range(batches))
+
     regions = [(0, None), (None, 0), (1, None), (None, 1), (2, None)]
-    regions += [(k, k - 1) for k in range(3, chunks)] + [(None, chunks - 1)]
+    regions += [(k, k - 1) for k in range(3, chunks - 1)]
+    regions += [(None, chunks - 2), (chunks - 1, None), (None, chunks - 1)]
     plan = [
-        (lambda _: bias_rs0(), {0: 10}),
-        (lambda _: bias_rs1(), {0: 11}),
+        (lambda _: bias_rs0(), {0: 11}),
+        (lambda _: bias_rs1(), {0: 12}),
         (ag2, {1: 0, 2: 1, 3: 2, 4: 3, 5: 5}),
         (ag1, {3: 0, 4: 1, 5: 3}),
         (ag3, {1: 1, 2: 3, 3: 4, 4: 5, 5: 6}),
         (at3, {6: 7, 7: 8}),
         (atz, {6: 0, 7: 4}),
-        (rs4, {0: 9, 1: 10}),
-        (rs3, {0: 8, 1: 9, 2: 10}),
-        (rs2, {0: 7, 1: 8, 2: 9, 3: 10, 4: 11}),
-        (rs1, {0: 5, 1: 6, 2: 7, 3: 8, 4: 9, 5: 10, 6: 11}),
+        (rs4, {0: 10, 1: 12}),
+        (rs3, {0: 8.5, 1: 9, 2: 10, 3: 11, 4: 12}),
+        (rs2, {0: 7, 1: 7.5, 2: 8, 3: 9, 4: 10, 5: 12}),
+        (rs1, {0: 5.5, 1: 6, 2: 6.5, 3: 7, 4: 8, 5: 9, 6: 10}),
     ]
-    regions.append((None, None))
+
+    def ahead_of(at):
+        return [(stage, k) for stage, when in plan for k, ahead in when.items() if ahead == at]
+
+    def opening(j, carry):
+        for place in range(2):
+            for step in range(2):
+                for stage, k in ahead_of(2 * step + place):
+                    pl.when(j == step)(functools.partial(stage, k))
+            if place == 0:
+                forward_region(j)
+                region(lambda: forward(j, whole))
+            else:
+                region(lambda: weight_other(j))
+                reduce_c(j).start()
+                region(lambda: weight_own(j))
+        return carry
+
+    lax.fori_loop(0, 2, opening, 0)
     for at, (f, w) in enumerate(regions):
-        for stage, when in plan:
-            for k, ahead in when.items():
-                if ahead == at:
-                    stage(k)
+        if at < 4:
+            continue
+        for stage, k in ahead_of(at):
+            stage(k)
         if f is not None:
             forward_region(f)
         if w is not None:
             weight_region(w)
-        if f is None and w is None:
-            continue
+        merged = f is not None and w is not None
 
         @region
-        def _(f=f, w=w):
+        def _(f=f, w=w, merged=merged):
             if f is not None:
-                forward(f)
+                forward(f, whole[:1] if merged else whole)
             if w is not None:
-                weight_terms(w)
+                weight_other(w)
 
         if w is not None:
             reduce_c(w).start()
+            for stage, k in ahead_of(at + 0.5):
+                stage(k)
+
+            @region
+            def _(f=f, w=w, merged=merged):
+                if merged:
+                    forward(f, whole[1:])
+                weight_own(w)
+
+    for stage, k in ahead_of(len(regions)):
+        stage(k)
 
     def feature_grad(i):
         n, m = lax.div(i, first), lax.rem(i, first)
@@ -624,10 +657,10 @@
     late = [
         (rs1, {7: 0}),
         (lambda _: bias_rs2(), {0: 1}),
-        (rs2, {5: 1, 6: 2, 7: 4}),
-        (rs3, {3: 0, 4: 2, 5: 4, 6: 5, 7: 6}),
-        (lambda _: bias_rs3(), {0: 5}),
-        (rs4, {2: 1, 3: 3, 4: 5, 5: 7, 6: 7, 7: 7}),
+        (rs2, {6: 1, 7: 3}),
+        (rs3, {5: 1, 6: 4, 7: 5}),
+        (lambda _: bias_rs3(), {0: 3}),
+        (rs4, {2: 0, 3: 1, 4: 3, 5: 5, 6: 7, 7: 7}),
         (lambda _: bias_rs4(), {0: 7}),
     ]
 
@@ -695,7 +728,7 @@
         vmem((2, batches, local, CHUNK), BF16),
         vmem((SLOTS, A, B, Y, rows, CHUNK), F32),
         vmem((2, A, B, Y, rows, CHUNK), BF16),
-        vmem((chunks, A, B, Y, rows, CHUNK), BF16),
+        vmem((RECEIVED, A, B, Y, rows, CHUNK), BF16),
         vmem((2, Y - 1, A, B, rows, LANES), BF16),
         vmem((2, B - 1, A, Y, rows, LANES), BF16),
         vmem((2, B - 1, A, rows, LANES), BF16),

time: 99.4 us -> 96.3 us (0.969)
  Pallas kernels: 98.4 us -> 95.3 us
    pallas_call x1, Pallas kernels: 89.9 us -> 86.9 us  [per_device(): pl.pallas_call(functools.partial(kernel, dims), out_shape=kept, in_specs=...]
where the time goes in v1:
time: 96.3 us; the launch traced here: 96.1 us
  Pallas kernels  95.3 us (99%)
    pallas_call x1, Pallas kernels, per_device(): pl.pallas_call(functools.partial(kernel, dims), out_shape=kept, in_specs=...  86.9 us
    pallas_call x1, Pallas kernels, per_device(): pl.pallas_call(functools.partial(finish, dims), out_shape=[jax.ShapeDtype...  8.42 us

profile of v1, /device:TPU:0, one launch (start us, length us, event | category | flops | bytes accessed | tf_op | source)
XLA Modules:
  0.0 96.1 jit_solution(13351274102282560671)
XLA Ops:
  0.6 86.9 %shard_map.102 = (bf16[8,3,640,256]{3,2,1,0:T(8,128)(2,1)S(1)}, bf16[8,2,4,2,2,2,64,128]{7,6,5,4,3,2,1,0:T(8,128)(2,1)S(1)}, bf16[640,2048]{1,0:T(8,128)(2,1)S(1...) custom-call(bf16[3,640,2048]{2,1,0:T(8,128)(2,1)} %feat.1, ...), custom_call_target="tpu_custom_call" | custom-call | flops 48318382080 | bytes 31457280 | tf_op jit(solution)/shard_map/pallas_call | solution.py:791
  87.5 8.4 %shard_map.103 = (bf16[3,640,2048]{2,1,0:T(8,128)(2,1)}, bf16[3,640,2048]{2,1,0:T(8,128)(2,1)}, f32[64,2048]{1,0:T(8,128)}, f32[1,64]{1,0:T(1,128)}) custom-call(bf16[8,3,640,256]{3,2,1,0:T(8,128)(2,1)S(1)} %get-tuple-element.16.act, bf16[8,2,4,2,2,2,64,128]{7,6,5,4,3,2,1,0:T(8,128)(2,1)S(1)} %get-tuple-element.17.wg, ...), custom_call_target="tpu_custom_call" | custom-call | tf_op jit(solution)/shard_map/pallas_call | solution.py:804

commit v2 on v1

--- a/solution.py
+++ b/solution.py
@@ -85,7 +85,7 @@
     in_sem, ct_sem,
     gz_s, gz_r, g1a_s, g1a_r, g1b_s, g1b_r, g2a_s, g2a_r, g2b_s, g2b_r, gc_s, gc_r,
     rc_s, rc_r, p1a_s, p1a_r, p1b_s, p1b_r, p2a_s, p2a_r, p2b_s, p2b_r, pz_s, pz_r,
-    bz_s, bz_r, b1_s, b1_r, b2_s, b2_r, bc_s, bc_r, dc_s, dc_r, d1_s, d1_r, d2_s, d2_r, dz_s, dz_r,
+    ha_r, hb_r, bz_s, bz_r, b1_s, b1_r, b2_s, b2_r, bc_s, bc_r, dc_s, dc_r, d1_s, d1_r, d2_s, d2_r, dz_s, dz_r,
 ):
     A, B, Y, C = dims
     batches, local, D = feat.shape
@@ -213,6 +213,43 @@
         for d, dev in to_a:
             out.append(remote(ref, ref, gz_s.at[1], gz_r.at[k], dev))
         return out
+
+    def half_step(mine):
+        out = []
+        for d, dev in to_y:
+            ref = wg.at[0, 0, :, b, y if mine else down(y, d, Y), c]
+            out.append(remote(ref, ref, g2a_s.at[0, d - 1], ha_r.at[d - 1], dev))
+        for d, dev in to_b:
+            ref = wg.at[0, 1, :, b if mine else down(b, d, B), y, c]
+            out.append(remote(ref, ref, g2b_s.at[0, d - 1], hb_r.at[d - 1], dev))
+        return out
+
+    def ag2a():
+        for copy in half_step(True):
+            copy.start()
+
+    def ag2b():
+        for copy in gather_1(0, False):
+            copy.wait_recv()
+        for d, dev in to_y:
+            for e in range(1, B):
+                ref = wg.at[0, 0, :, down(b, e, B), y, c]
+                remote(ref, ref, g2a_s.at[0, d - 1], g2a_r.at[0, d - 1], dev).start()
+        for d, dev in to_b:
+            for e in range(1, Y):
+                ref = wg.at[0, 1, :, b, down(y, e, Y), c]
+                remote(ref, ref, g2b_s.at[0, d - 1], g2b_r.at[0, d - 1], dev).start()
+
+    def ag3_first():
+        for copy in half_step(False):
+            copy.wait_recv()
+        for d, dev in to_y:
+            ref = wg.at[0, 0, :, : B - 1, y, c]
+            remote(ref, ref, g2a_s.at[0, d - 1], g2a_r.at[0, d - 1], dev).wait_recv()
+        for d, dev in to_b:
+            ref = wg.at[0, 1, :, b, : Y - 1, c]
+            remote(ref, ref, g2b_s.at[0, d - 1], g2b_r.at[0, d - 1], dev).wait_recv()
+        gather_c(0, True).start()
 
     def gather_c(k, mine):
         ref = wg.at[k, :, :, :, :, c if mine else oc]
@@ -345,8 +382,9 @@
     early = {
         2: [lambda: agz(1)],
         4: [bias_ag1, lambda: ag1(0)],
-        6: [lambda: at2(6), lambda: at2(7), lambda: agz(2)],
-        10: [bias_ag2, lambda: ag2(0), lambda: ag1(1), lambda: agz(3)],
+        6: [ag2a, lambda: agz(2)],
+        8: [lambda: at2(6), lambda: at2(7)],
+        10: [bias_ag2, ag2b, lambda: ag1(1), lambda: agz(3)],
     }
     for m in range(batches):
         feat_loads[m].wait()
@@ -368,7 +406,7 @@
     agz(4)
     ag1(2)
     bias_ag3()
-    ag3(0)
+    ag3_first()
     agz(5)
 
     bias_c(False).wait_recv()
@@ -587,7 +625,7 @@
     regions += [(None, chunks - 2), (chunks - 1, None), (None, chunks - 1)]
     plan = [
         (lambda _: bias_rs0(), {0: 11}),
-        (lambda _: bias_rs1(), {0: 12}),
+        (lambda _: bias_rs1(), {0: 11.5}),
         (ag2, {1: 0, 2: 1, 3: 2, 4: 3, 5: 5}),
         (ag1, {3: 0, 4: 1, 5: 3}),
         (ag3, {1: 1, 2: 3, 3: 4, 4: 5, 5: 6}),
@@ -656,10 +694,10 @@
 
     late = [
         (rs1, {7: 0}),
+        (rs2, {6: 0, 7: 2}),
         (lambda _: bias_rs2(), {0: 1}),
-        (rs2, {6: 1, 7: 3}),
-        (rs3, {5: 1, 6: 4, 7: 5}),
         (lambda _: bias_rs3(), {0: 3}),
+        (rs3, {5: 1, 6: 3, 7: 4}),
         (rs4, {2: 0, 3: 1, 4: 3, 5: 5, 6: 7, 7: 7}),
         (lambda _: bias_rs4(), {0: 7}),
     ]
@@ -754,6 +792,7 @@
         dma((4 + batches,)),
         dma((2,)),
     ]
+    scratch_tail = [dma((Y - 1,)), dma((B - 1,))]
     for sent, received in (
         ((2,), (chunks,)),
         ((2, B - 1), (chunks, B - 1)),
@@ -767,6 +806,7 @@
         ((2, B - 1), (chunks, B - 1)),
         ((2, Y - 1), (chunks, Y - 1)),
         ((2,), (chunks,)),
+        (None, scratch_tail),
         ((1,), (1,)),
         ((B - 1,), (B - 1,)),
         ((Y - 1,), (Y - 1,)),
@@ -776,7 +816,7 @@
         ((B - 1,), (B - 1,)),
         ((1,), (1,)),
     ):
-        scratch += [dma(sent), dma(received)]
+        scratch += received if sent is None else [dma(sent), dma(received)]
     vmem_spec = pl.BlockSpec(memory_space=pltpu.VMEM)
     kept = [
         vmem((chunks, batches, local, CHUNK), BF16),

time: 96.3 us -> 95.2 us (0.989)
  Pallas kernels: 95.3 us -> 94.2 us
    pallas_call x1, Pallas kernels: 86.9 us -> 85.8 us  [per_device(): pl.pallas_call(functools.partial(kernel, dims), out_shape=kept, in_specs=...]
where the time goes in v2:
time: 95.2 us; the launch traced here: 95.1 us
  Pallas kernels  94.2 us (99%)
    pallas_call x1, Pallas kernels, per_device(): pl.pallas_call(functools.partial(kernel, dims), out_shape=kept, in_specs=...  85.8 us
    pallas_call x1, Pallas kernels, per_device(): pl.pallas_call(functools.partial(finish, dims), out_shape=[jax.ShapeDtype...  8.42 us

profile of v2, /device:TPU:0, one launch (start us, length us, event | category | flops | bytes accessed | tf_op | source)
XLA Modules:
  0.0 95.1 jit_solution(9387815322366642917)
XLA Ops:
  0.6 85.8 %shard_map.102 = (bf16[8,3,640,256]{3,2,1,0:T(8,128)(2,1)S(1)}, bf16[8,2,4,2,2,2,64,128]{7,6,5,4,3,2,1,0:T(8,128)(2,1)S(1)}, bf16[640,2048]{1,0:T(8,128)(2,1)S(1...) custom-call(bf16[3,640,2048]{2,1,0:T(8,128)(2,1)} %feat.1, ...), custom_call_target="tpu_custom_call" | custom-call | flops 48318382080 | bytes 31457280 | tf_op jit(solution)/shard_map/pallas_call | solution.py:831
  86.5 8.4 %shard_map.103 = (bf16[3,640,2048]{2,1,0:T(8,128)(2,1)}, bf16[3,640,2048]{2,1,0:T(8,128)(2,1)}, f32[64,2048]{1,0:T(8,128)}, f32[1,64]{1,0:T(1,128)}) custom-call(bf16[8,3,640,256]{3,2,1,0:T(8,128)(2,1)S(1)} %get-tuple-element.16.act, bf16[8,2,4,2,2,2,64,128]{7,6,5,4,3,2,1,0:T(8,128)(2,1)S(1)} %get-tuple-element.17.wg, ...), custom_call_target="tpu_custom_call" | custom-call | tf_op jit(solution)/shard_map/pallas_call | solution.py:844

commit v3 on v2

--- a/solution.py
+++ b/solution.py
@@ -631,10 +631,10 @@
         (ag3, {1: 1, 2: 3, 3: 4, 4: 5, 5: 6}),
         (at3, {6: 7, 7: 8}),
         (atz, {6: 0, 7: 4}),
-        (rs4, {0: 10, 1: 12}),
+        (rs4, {0: 11, 1: 12}),
         (rs3, {0: 8.5, 1: 9, 2: 10, 3: 11, 4: 12}),
-        (rs2, {0: 7, 1: 7.5, 2: 8, 3: 9, 4: 10, 5: 12}),
-        (rs1, {0: 5.5, 1: 6, 2: 6.5, 3: 7, 4: 8, 5: 9, 6: 10}),
+        (rs2, {0: 7, 1: 7.5, 2: 8, 3: 9, 4: 10, 5: 11.5}),
+        (rs1, {0: 5.5, 1: 6, 2: 6.5, 3: 7, 4: 8, 5: 9, 6: 10, 7: 12}),
     ]
 
     def ahead_of(at):
@@ -693,7 +693,6 @@
         pool_e[part, cols] = feature_tile(dims, wg, gp_e, adj_e, scale_e, local, n, m)
 
     late = [
-        (rs1, {7: 0}),
         (rs2, {6: 0, 7: 2}),
         (lambda _: bias_rs2(), {0: 1}),
         (lambda _: bias_rs3(), {0: 3}),

time: 95.2 us -> 94.5 us (level)
  no operation moved by 1% of the time
where the time goes in v3:
time: 94.5 us; the launch traced here: 94.3 us
  Pallas kernels  93.5 us (99%)
    pallas_call x1, Pallas kernels, per_device(): pl.pallas_call(functools.partial(kernel, dims), out_shape=kept, in_specs=...  85.1 us
    pallas_call x1, Pallas kernels, per_device(): pl.pallas_call(functools.partial(finish, dims), out_shape=[jax.ShapeDtype...  8.41 us

profile of v3, /device:TPU:0, one launch (start us, length us, event | category | flops | bytes accessed | tf_op | source)
XLA Modules:
  0.0 94.3 jit_solution(7565778367791107636)
XLA Ops:
  0.6 85.1 %shard_map.102 = (bf16[8,3,640,256]{3,2,1,0:T(8,128)(2,1)S(1)}, bf16[8,2,4,2,2,2,64,128]{7,6,5,4,3,2,1,0:T(8,128)(2,1)S(1)}, bf16[640,2048]{1,0:T(8,128)(2,1)S(1...) custom-call(bf16[3,640,2048]{2,1,0:T(8,128)(2,1)} %feat.1, ...), custom_call_target="tpu_custom_call" | custom-call | flops 48318382080 | bytes 31457280 | tf_op jit(solution)/shard_map/pallas_call | solution.py:830
  85.7 8.4 %shard_map.103 = (bf16[3,640,2048]{2,1,0:T(8,128)(2,1)}, bf16[3,640,2048]{2,1,0:T(8,128)(2,1)}, f32[64,2048]{1,0:T(8,128)}, f32[1,64]{1,0:T(1,128)}) custom-call(bf16[8,3,640,256]{3,2,1,0:T(8,128)(2,1)S(1)} %get-tuple-element.16.act, bf16[8,2,4,2,2,2,64,128]{7,6,5,4,3,2,1,0:T(8,128)(2,1)S(1)} %get-tuple-element.17.wg, ...), custom_call_target="tpu_custom_call" | custom-call | tf_op jit(solution)/shard_map/pallas_call | solution.py:843

commit v4 on v3

--- a/solution.py
+++ b/solution.py
@@ -649,9 +649,13 @@
                 forward_region(j)
                 region(lambda: forward(j, whole))
             else:
-                region(lambda: weight_other(j))
+
+                @region
+                def _():
+                    weight_other(j)
+                    weight_own(j)
+
                 reduce_c(j).start()
-                region(lambda: weight_own(j))
         return carry
 
     lax.fori_loop(0, 2, opening, 0)

time: 94.5 us -> 94.2 us (level)
  no operation moved by 1% of the time
where the time goes in v4:
time: 94.2 us; the launch traced here: 94.1 us
  Pallas kernels  93.2 us (99%)
    pallas_call x1, Pallas kernels, per_device(): pl.pallas_call(functools.partial(kernel, dims), out_shape=kept, in_specs=...  84.8 us
    pallas_call x1, Pallas kernels, per_device(): pl.pallas_call(functools.partial(finish, dims), out_shape=[jax.ShapeDtype...  8.41 us

profile of v4, /device:TPU:0, one launch (start us, length us, event | category | flops | bytes accessed | tf_op | source)
XLA Modules:
  0.0 94.1 jit_solution(9867561637027152532)
XLA Ops:
  0.6 84.8 %shard_map.102 = (bf16[8,3,640,256]{3,2,1,0:T(8,128)(2,1)S(1)}, bf16[8,2,4,2,2,2,64,128]{7,6,5,4,3,2,1,0:T(8,128)(2,1)S(1)}, bf16[640,2048]{1,0:T(8,128)(2,1)S(1...) custom-call(bf16[3,640,2048]{2,1,0:T(8,128)(2,1)} %feat.1, ...), custom_call_target="tpu_custom_call" | custom-call | flops 48318382080 | bytes 31457280 | tf_op jit(solution)/shard_map/pallas_call | solution.py:834
  85.5 8.4 %shard_map.103 = (bf16[3,640,2048]{2,1,0:T(8,128)(2,1)}, bf16[3,640,2048]{2,1,0:T(8,128)(2,1)}, f32[64,2048]{1,0:T(8,128)}, f32[1,64]{1,0:T(1,128)}) custom-call(bf16[8,3,640,256]{3,2,1,0:T(8,128)(2,1)S(1)} %get-tuple-element.16.act, bf16[8,2,4,2,2,2,64,128]{7,6,5,4,3,2,1,0:T(8,128)(2,1)S(1)} %get-tuple-element.17.wg, ...), custom_call_target="tpu_custom_call" | custom-call | tf_op jit(solution)/shard_map/pallas_call | solution.py:847
